TPU v7x, 32 devices: a whole 2x2x4 slice. The times are simulated.
32 devices in a mesh: groups: 2 (over y), state: 4 (over z), dp: 2 (over x), sub: 2 (over core).
Axes of the slice: x: 2, y: 2, z: 4, core: 2. Of those that a mesh axis runs over, the one named last changes fastest.
Arguments:
- transition: bfloat16 [4, 4, 1024, 16384], P(None, 'state', None, ('dp', 'sub')), may hold values from 0 to 55, as said below
- emission: bfloat16 [4, 512, 4, 4, 1024], P(None, 'groups', ('dp', 'sub')), parts along dimension 1, may hold values from 0 to 1100, as said below
- start: float32 [512, 4, 4, 1024], P('groups', ('dp', 'sub'), 'state'), parts along dimension 0, may hold values from 0.1 to 10
Outputs:
- messages: float32 [4, 512, 4, 4, 1024], P(None, 'groups', ('dp', 'sub'), 'state'), parts along dimension 1
- log_scale: float32 [512], P('groups'), parts along dimension 0
There are 2 independent parts, one for each index of `groups`. A program takes and returns all parts, laid end to end along the dimension named above; an argument that names none is the same for every part. Nothing has to cross between parts.
Inputs may be any that keep to these rules, and one draw needn't show every extreme that they name: `transition`: positive. `emission`: positive.
All inputs are finite; a program needn't handle non-finite values.
Results may differ from a plain program's by a relative error of at most 0.00057.
Values may be sent and summed in bfloat16 or wider, within the bound.
No kernel may reach another device: no remote copies, remote signals or barrier semaphores. Data moves between devices by JAX's collectives and lax.ppermute only.
A program may use at most 192 MiB of HBM per device.

v0:
```python
import jax
import jax.numpy as jnp
from jax import lax
from jax.sharding import PartitionSpec as P

H = 16384
STEPS = 4


def shards(transition, emission, start):
    seq_count = start.shape[0]
    piece_len = start.shape[3]
    blocks = lax.axis_size("state")
    col_width = transition.shape[3]
    own_row = lax.axis_index("state")
    message = start
    history = []
    log_parts = []
    for step_idx in range(STEPS):
        lowered = message.astype(jnp.bfloat16)
        shard_rows = lax.all_gather(lowered, ("dp", "sub"), axis=1, tiled=True)
        num_rows = shard_rows.shape[1]
        weight_rows = transition
        weight_rows = weight_rows.reshape(num_rows * piece_len, col_width)
        left_side = shard_rows.reshape(seq_count, num_rows * piece_len)
        mixed = jnp.dot(left_side, weight_rows, preferred_element_type=jnp.float32)
        step_weights = emission[step_idx]
        summed = lax.psum_scatter(
            mixed.reshape(seq_count, blocks, piece_len), "state", scatter_dimension=1, tiled=True
        )
        own_weights = lax.dynamic_index_in_dim(step_weights, own_row, 2, keepdims=True)
        weighted = summed.reshape(seq_count, 1, 1, piece_len) * own_weights.astype(jnp.float32)
        normal_sum = lax.psum(jnp.sum(weighted, axis=(1, 2, 3)), ("state", "dp", "sub")) / H
        message = weighted / normal_sum[:, None, None, None]
        log_parts.append(jnp.log(normal_sum))
        history.append(message)
    log_local = log_parts[0]
    for extra in log_parts[1:]:
        log_local = log_local + extra
    return (jnp.stack(history), log_local)


def solution(mesh):
    in_specs = (
        P(None, "state", None, ("dp", "sub")),
        P(None, "groups", ("dp", "sub"), None, None),
        P("groups", ("dp", "sub"), "state", None),
    )
    out_specs = (P(None, "groups", ("dp", "sub"), "state", None), P("groups"))
    return jax.shard_map(shards, mesh=mesh, in_specs=in_specs, out_specs=out_specs, check_vma=False)
```

profile of v0, /device:TPU:0, one launch (start us, length us, event | category | flops | bytes accessed | tf_op | source)
XLA Modules:
  0.0 683.2 jit_solution(9521364947443854474)
XLA Ops:
  7.2 2.9 convert_element_type.148
  10.2 41.0 %copy.23 = bf16[4096,4096]{1,0:T(8,128)(2,1)} copy(bf16[4096,4096]{0,1:T(8,128)(2,1)} %bitcast.83) | data formatting | bytes 67108864 | tf_op jit(solution)/shard_map/dot_general | solution.py:26
  51.2 14.1 %reduce.4 = bf16[256,4,1024]{2,1,0:T(4,128)(2,1)S(1)} reduce(bf16[256,4,1,1024]{3,2,1,0:T(2,128)(2,1)} %all-gather.5.cloned.1.call-done, bf16[]{:T(256)} %constant.32), dimensions={2}, to_apply=%all_gather.12.reduce_sub_computation | reduce | bytes 4194306 | tf_op jit(solution)/shard_map/all_gather | solution.py:21
  68.1 17.6 %fusion.22 = f32[256,4,1024]{2,0,1:T(8,128)} fusion(bf16[256,4096,1]{1,0,2:T(8,128)(2,1)} %reshape.330, bf16[4,1024,4096]{2,1,0:T(8,128)(2,1)} %bitcast.84), kind=kOutput, calls=%fused_computation.43 | convolution fusion | flops 8589934592 | bytes 39845888 | tf_op jit(solution)/shard_map/dot_general | solution.py:26
  85.8 6.4 fusion.21
  93.2 75.1 %reduce-scatter.5.cloned.1.call-done = f32[256,1,1024]{2,0,1:T(8,128)} async-done(((f32[256,4,1024]{2,0,1:T(8,128)}), f32[256,1,1024]{2,0,1:T(8,128)}) %reduce-scatter.5.cloned.1.call-update) | async-done | bytes 1048592 | tf_op jit(solution)/shard_map/reduce_scatter | solution.py:28
  169.8 32.7 %psum.28 = f32[256]{0:T(256)S(1)} all-reduce(f32[256]{0:T(256)S(1)} %fusion.5), channel_id=1, replica_groups=mesh['groups'=2,'state'=4,'dp'=2,'sub'=2] {'state','dp','sub'}, use_global_device_ids=true, to_apply=%region_2.3 | all-reduce | flops 256 | bytes 2048 | tf_op jit(solution)/shard_map/psum | solution.py:33
  205.1 19.7 %all-gather.7.cloned.1.call-done = bf16[256,4,1,1024]{3,0,2,1:T(8,128)(2,1)} async-done(((bf16[256,1,1,1024]{3,0,2,1:T(8,128)(2,1)}), bf16[256,4,1,1024]{3,0,2,1:T(8,128)(2,1)}) %all-gather.7.cloned.1.call-update) | async-done | bytes 2097168 | tf_op jit(solution)/shard_map/all_gather | solution.py:21
  224.8 2.8 copy.25
  227.7 17.2 %fusion.23 = f32[256,4,1024]{2,0,1:T(8,128)} fusion(bf16[256,4096,1]{0,1,2:T(8,128)(2,1)S(1)} %bitcast.89, bf16[4,1024,4096]{2,1,0:T(8,128)(2,1)} %bitcast.85), kind=kOutput, calls=%fused_computation.44 | convolution fusion | flops 8589934592 | bytes 39845888 | tf_op jit(solution)/shard_map/dot_general | solution.py:26
  247.7 74.2 %reduce-scatter.7.cloned.1.call-done = f32[256,1,1024]{2,0,1:T(8,128)} async-done(((f32[256,4,1024]{2,0,1:T(8,128)}), f32[256,1,1024]{2,0,1:T(8,128)}) %reduce-scatter.7.cloned.1.call-update) | async-done | bytes 1048592 | tf_op jit(solution)/shard_map/reduce_scatter | solution.py:28
  323.4 32.7 %psum.29 = f32[256]{0:T(256)S(1)} all-reduce(f32[256]{0:T(256)S(1)} %fusion.11), channel_id=1, replica_groups=mesh['groups'=2,'state'=4,'dp'=2,'sub'=2] {'state','dp','sub'}, use_global_device_ids=true, to_apply=%region_5.6 | all-reduce | flops 256 | bytes 2048 | tf_op jit(solution)/shard_map/psum | solution.py:33
  358.5 19.9 %all-gather.9.cloned.1.call-done = bf16[256,4,1,1024]{3,0,2,1:T(8,128)(2,1)} async-done(((bf16[256,1,1,1024]{3,0,2,1:T(8,128)(2,1)}), bf16[256,4,1,1024]{3,0,2,1:T(8,128)(2,1)}) %all-gather.9.cloned.1.call-update) | async-done | bytes 2097168 | tf_op jit(solution)/shard_map/all_gather | solution.py:21
  378.4 3.9 copy.28
  382.4 17.7 %fusion.24 = f32[256,4,1024]{2,0,1:T(8,128)} fusion(bf16[256,4096,1]{0,1,2:T(8,128)(2,1)} %bitcast.90, bf16[4,1024,4096]{2,1,0:T(8,128)(2,1)} %bitcast.86), kind=kOutput, calls=%fused_computation.45 | convolution fusion | flops 8589934592 | bytes 39845888 | tf_op jit(solution)/shard_map/dot_general | solution.py:26
  402.8 74.2 %reduce-scatter.9.cloned.1.call-done = f32[256,1,1024]{2,0,1:T(8,128)} async-done(((f32[256,4,1024]{2,0,1:T(8,128)}), f32[256,1,1024]{2,0,1:T(8,128)}) %reduce-scatter.9.cloned.1.call-update) | async-done | bytes 1048592 | tf_op jit(solution)/shard_map/reduce_scatter | solution.py:28
  478.5 32.7 %psum.30 = f32[256]{0:T(256)S(1)} all-reduce(f32[256]{0:T(256)S(1)} %fusion.17), channel_id=1, replica_groups=mesh['groups'=2,'state'=4,'dp'=2,'sub'=2] {'state','dp','sub'}, use_global_device_ids=true, to_apply=%region_8.9 | all-reduce | flops 256 | bytes 2048 | tf_op jit(solution)/shard_map/psum | solution.py:33
  513.8 19.7 %all-gather.11.cloned.1.call-done = bf16[256,4,1,1024]{3,0,2,1:T(8,128)(2,1)} async-done(((bf16[256,1,1,1024]{3,0,2,1:T(8,128)(2,1)}), bf16[256,4,1,1024]{3,0,2,1:T(8,128)(2,1)}) %all-gather.11.cloned.1.call-update) | async-done | bytes 2097168 | tf_op jit(solution)/shard_map/all_gather | solution.py:21
  533.5 3.9 copy.31
  537.5 17.7 %fusion.25 = f32[256,4,1024]{2,0,1:T(8,128)} fusion(bf16[256,4096,1]{0,1,2:T(8,128)(2,1)} %bitcast.88, bf16[4,1024,4096]{2,1,0:T(8,128)(2,1)} %bitcast.87), kind=kOutput, calls=%fused_computation.46 | convolution fusion | flops 8589934592 | bytes 39845888 | tf_op jit(solution)/shard_map/dot_general | solution.py:26
  555.2 3.8 constant_dynamic-slice_fusion
  564.2 67.9 %reduce-scatter.11.cloned.1.call-done = f32[256,1,1024]{2,0,1:T(8,128)} async-done(((f32[256,4,1024]{2,0,1:T(8,128)}), f32[256,1,1024]{2,0,1:T(8,128)}) %reduce-scatter.11.cloned.1.call-update) | async-done | bytes 1048592 | tf_op jit(solution)/shard_map/reduce_scatter | solution.py:28
  633.6 32.7 %psum.31 = f32[256]{0:T(256)S(1)} all-reduce(f32[256]{0:T(256)S(1)} %fusion.2), channel_id=1, replica_groups=mesh['groups'=2,'state'=4,'dp'=2,'sub'=2] {'state','dp','sub'}, use_global_device_ids=true, to_apply=%region_11.12 | all-reduce | flops 256 | bytes 2048 | tf_op jit(solution)/shard_map/psum | solution.py:33
  670.0 6.3 copy.34
  (47 shorter events, 32.1 us)
Async XLA Ops:
  7.2 44.1 %all-gather.5.cloned.1.call-start = ((), (), s32[]{:S(2)}) async-start(), calls=%async_computation.4 | async-start | bytes 5242880 | tf_op jit(solution)/shard_map/all_gather | solution.py:21
  10.1 158.1 %reduce-scatter.5.cloned.1.call-start = ((), (), s32[]{:S(2)}) async-start(), calls=%async_computation.5 | async-start | bytes 5242880 | tf_op jit(solution)/shard_map/reduce_scatter | solution.py:28
  85.7 139.1 %all-gather.7.cloned.1.call-start = ((), (), s32[]{:S(2)}) async-start(), calls=%async_computation.6 | async-start | bytes 2621440 | tf_op jit(solution)/shard_map/all_gather | solution.py:21
  204.9 117.0 %reduce-scatter.7.cloned.1.call-start = ((), (), s32[]{:S(2)}) async-start(), calls=%async_computation.7 | async-start | bytes 5242880 | tf_op jit(solution)/shard_map/reduce_scatter | solution.py:28
  245.0 133.5 %all-gather.9.cloned.1.call-start = ((), (), s32[]{:S(2)}) async-start(), calls=%async_computation.8 | async-start | bytes 2621440 | tf_op jit(solution)/shard_map/all_gather | solution.py:21
  358.5 118.5 %reduce-scatter.9.cloned.1.call-start = ((), (), s32[]{:S(2)}) async-start(), calls=%async_computation.9 | async-start | bytes 5242880 | tf_op jit(solution)/shard_map/reduce_scatter | solution.py:28
  400.1 133.5 %all-gather.11.cloned.1.call-start = ((), (), s32[]{:S(2)}) async-start(), calls=%async_computation.10 | async-start | bytes 2621440 | tf_op jit(solution)/shard_map/all_gather | solution.py:21
  513.6 118.5 %reduce-scatter.11.cloned.1.call-start = ((), (), s32[]{:S(2)}) async-start(), calls=%async_computation.11 | async-start | bytes 5242880 | tf_op jit(solution)/shard_map/reduce_scatter | solution.py:28
  555.2 6.4 copy-start
  555.2 7.7 %copy-start.1 = (f32[256,1,1024]{2,0,1:T(8,128)S(1)}, f32[256,1,1024]{2,0,1:T(8,128)}, u32[]{:S(2)}) copy-start(f32[256,1,1024]{2,0,1:T(8,128)} %reduce-scatter.9.cloned.1.call-done) | copy-start | bytes 3145732
  561.6 70.5 %copy-start.2 = (bf16[1,256,1,1,1024]{4,3,2,1,0:T(2,128)(2,1)S(1)}, bf16[1,256,1,1,1024]{4,3,2,1,0:T(2,128)(2,1)}, u32[]{:S(2)}) copy-start(bf16[1,256,1,1,1024]{4,3,2,1,0:T(2,128)(2,1)} %constant_dynamic-slice_fusion) | copy-start | bytes 1572868
  562.9 105.5 %copy-start.3 = (f32[1,256,1,1,1024]{4,1,3,2,0:T(8,128)S(1)}, f32[1,256,1,1,1024]{4,1,3,2,0:T(8,128)}, u32[]{:S(2)}) copy-start(f32[1,256,1,1,1024]{4,1,3,2,0:T(8,128)} %fusion.3) | copy-start | bytes 3145732
  564.2 104.2 %copy-start.4 = (f32[1,256,1,1,1024]{4,1,3,2,0:T(8,128)S(1)}, f32[1,256,1,1,1024]{4,1,3,2,0:T(8,128)}, u32[]{:S(2)}) copy-start(f32[1,256,1,1,1024]{4,1,3,2,0:T(8,128)} %fusion.9) | copy-start | bytes 3145732
Sparse Core Ops, SparseCore 0:
  10.3 37.7 all-gather.4
  85.9 82.3 reduce-scatter.4
  205.0 19.8 all-gather.6
  245.1 76.7 reduce-scatter.6
  358.6 19.8 all-gather.8
  400.2 76.7 reduce-scatter.8
  513.7 19.8 all-gather.10
  555.3 76.7 reduce-scatter.10
where the time goes:
time: 685 us; the launch traced here: 683 us
  waiting for transfers between devices  351 us (51%)
  blocking collectives  131 us (19%)
  local copies, waits for them, and re-layouts  77.5 us (11%)
  matrix products  70.2 us (10%)
  other arithmetic  38.9 us (6%)
  between operations  14.2 us (2%)
    reduce_scatter x4, waiting for transfers between devices, shards(): lax.psum_scatter(mixed.reshape(seq_count, blocks, piece_len), 'state', sc...  291 us
    psum x4, blocking collectives, shards(): lax.psum(jnp.sum(weighted, axis=(1, 2, 3)), ('state', 'dp', 'sub')) / H  131 us
    dot_general x4, matrix products, shards(): mixed = jnp.dot(left_side, weight_rows, preferred_element_type=jnp.float32)  70.2 us
    all_gather x4, waiting for transfers between devices, shards(): shard_rows = lax.all_gather(lowered, ('dp', 'sub'), axis=1, tiled=True)  59.4 us
    dot_general x1, local copies, waits for them, and re-layouts, shards(): mixed = jnp.dot(left_side, weight_rows, preferred_element_type=jnp.float32)  41 us
    all_gather x1, other arithmetic, shards(): shard_rows = lax.all_gather(lowered, ('dp', 'sub'), axis=1, tiled=True)  14.1 us
  transfers between devices with their start and end apart: 8, of which 7 were waited for; matrix products, arithmetic and copies ran while one was open for 9% of the time, Pallas kernels for 0%

commit v1 on v0

v1 whole, which is shorter than its diff:
```python
import functools

import jax
import jax.numpy as jnp
from jax import lax
from jax.experimental import pallas as pl
from jax.experimental.pallas import tpu as pltpu
from jax.sharding import PartitionSpec as P

STEPS = 4
HALVES = 2
TOP = 60000.0
START_TOP = 10.0


def product_kernel(num_x, with_peak, idx_ref, *refs):
    x_refs, t_ref, out_ref = refs[:num_x], refs[num_x], refs[num_x + 1]
    depth = x_refs[0].shape[1]
    total = None
    for q in range(num_x):
        rows = pl.ds(pl.multiple_of(idx_ref[1 + q] * depth, depth), depth)
        term = jnp.dot(x_refs[q][...], t_ref[rows, :], preferred_element_type=jnp.float32)
        total = term if total is None else total + term
    out_ref[0] = total
    if with_peak:
        peak_ref = refs[num_x + 2]
        here = jnp.max(t_ref[...].astype(jnp.float32).reshape(-1, 8, t_ref.shape[1]), axis=0)
        first = jnp.logical_and(pl.program_id(0) == 0, pl.program_id(1) == 0)

        @pl.when(first)
        def _():
            peak_ref[...] = here

        @pl.when(jnp.logical_not(first))
        def _():
            peak_ref[...] = jnp.maximum(peak_ref[...], here)


def product(indices, xs, table, blocks, with_peak):
    seqs, depth = xs[0].shape
    rows, width = table.shape
    piece = width // blocks
    tile = min(512, piece)
    per = piece // tile

    def place(o, c, idx):
        return (0, lax.rem(idx[0] + o, blocks) * per + c)

    out_shape = [jax.ShapeDtypeStruct((blocks, seqs, piece), jnp.float32)]
    out_specs = [pl.BlockSpec((1, seqs, tile), lambda o, c, idx: (o, 0, c))]
    if with_peak:
        out_shape.append(jax.ShapeDtypeStruct((8, tile), jnp.float32))
        out_specs.append(pl.BlockSpec((8, tile), lambda o, c, idx: (0, 0)))
    return pl.pallas_call(
        functools.partial(product_kernel, len(xs), with_peak),
        grid_spec=pltpu.PrefetchScalarGridSpec(
            num_scalar_prefetch=1,
            grid=(blocks, per),
            in_specs=[pl.BlockSpec((seqs, depth), lambda o, c, idx: (0, 0)) for _ in xs]
            + [pl.BlockSpec((rows, tile), place)],
            out_specs=out_specs,
        ),
        out_shape=out_shape,
        compiler_params=pltpu.CompilerParams(vmem_limit_bytes=32 * 2**20),
        cost_estimate=pl.CostEstimate(
            flops=2 * seqs * rows * width, bytes_accessed=2 * rows * width, transcendentals=0
        ),
        name="product_peak" if with_peak else "product",
    )(indices, *xs, table)


def gather_blocks(block):
    dp, sub = lax.axis_size("dp"), lax.axis_size("sub")
    found = [block]
    for k in range(1, dp):
        found.append(lax.ppermute(block, "dp", [(i, (i + k) % dp) for i in range(dp)]))
    out = []
    for l in range(sub):
        for item in found:
            out.append(item if l == 0 else lax.ppermute(item, "sub", [(i, (i + l) % sub) for i in range(sub)]))
    return out


def block_owners():
    dp, sub = lax.axis_size("dp"), lax.axis_size("sub")
    x, c = lax.axis_index("dp"), lax.axis_index("sub")
    return [
        lax.rem(x + dp - k, dp) * sub + lax.rem(c + sub - l, sub) for l in range(sub) for k in range(dp)
    ]


def line_sum(parts, into, back, first_into, first_back_r, first_back_l):
    n = lax.axis_size("state")
    right = left = None
    for k in range(1, n):
        scale = first_into if k == 1 else into
        to_r, to_l = parts[n - k], parts[k]
        if k > 1:
            to_r = to_r + right.astype(jnp.float32) * (first_back_r if k == 2 else back)
            to_l = to_l + left.astype(jnp.float32) * (first_back_l if k == 2 else back)
        right = lax.ppermute((to_r * scale).astype(jnp.float16), "state", [(i, i + 1) for i in range(k)])
        left = lax.ppermute((to_l * scale).astype(jnp.float16), "state", [(i, i - 1) for i in range(n - k, n)])
    last_r, last_l = (first_back_r, first_back_l) if n == 2 else (back, back)
    return parts[0] + right.astype(jnp.float32) * last_r + left.astype(jnp.float32) * last_l


def shards(transition, emission, start):
    seq_count = start.shape[0]
    piece = start.shape[3]
    blocks = lax.axis_size("state")
    me = lax.axis_index("state")
    table = transition.reshape(transition.shape[0] * piece, transition.shape[3])
    hidden = blocks * piece * lax.axis_size("dp") * lax.axis_size("sub")
    half = seq_count // HALVES
    indices = jnp.stack([me] + block_owners()).astype(jnp.int32)
    weights = jnp.transpose(emission[:, :, 0], (0, 2, 1, 3))
    weights = jnp.concatenate([weights, weights], axis=1)
    weights = lax.dynamic_slice_in_dim(weights, me, blocks, 1)

    messages = [start[h * half : (h + 1) * half, 0, 0] for h in range(HALVES)]
    history, normals = [], []
    into = back = None
    for step in range(STEPS):
        step_messages, step_normals = [], []
        for h in range(HALVES):
            rows = slice(h * half, (h + 1) * half)
            xs = gather_blocks(messages[h].astype(jnp.bfloat16))
            first = step == 0 and h == 0
            if first:
                parts, peak = product(indices, xs, table, blocks, True)
                own_peak = jnp.max(peak)
                peaks = lax.all_gather(jnp.full((1, 128), own_peak), "state", axis=0, tiled=True)[:, 0]
                top_peak = jnp.max(peaks)
                into = TOP / (hidden * top_peak)
                back = hidden * top_peak / TOP
                peak_r = lax.dynamic_index_in_dim(peaks, lax.rem(me + blocks - 1, blocks), 0, False)
                peak_l = lax.dynamic_index_in_dim(peaks, lax.rem(me + 1, blocks), 0, False)
                spread = hidden * START_TOP
                scales = (
                    into / START_TOP, back * START_TOP,
                    TOP / (spread * own_peak), spread * peak_r / TOP, spread * peak_l / TOP,
                )
            else:
                (parts,) = product(indices, xs, table, blocks, False)
                grow = START_TOP if step == 0 else 1.0
                scales = (into / grow, back * grow, into / grow, back * grow, back * grow)
            step_weights = weights[step, :, rows].astype(jnp.float32)
            own_sum = jnp.sum(parts * step_weights, axis=(0, 2))
            sums = lax.all_gather(own_sum[None], ("state", "dp", "sub"), axis=0, tiled=True)
            normal = jnp.sum(sums, axis=0) / hidden
            summed = line_sum([parts[o] for o in range(blocks)], *scales)
            message = summed * step_weights[0] / normal[:, None]
            messages[h] = message
            step_messages.append(message)
            step_normals.append(normal)
        history.append(jnp.concatenate(step_messages, axis=0))
        normals.append(jnp.concatenate(step_normals, axis=0))
    log_scale = functools.reduce(lambda a, b: a + b, [jnp.log(x) for x in normals])
    out = jnp.stack(history).reshape(STEPS, seq_count, 1, 1, piece)
    return out, log_scale


def solution(mesh):
    in_specs = (
        P(None, "state", None, ("dp", "sub")),
        P(None, "groups", ("dp", "sub"), None, None),
        P("groups", ("dp", "sub"), "state", None),
    )
    out_specs = (P(None, "groups", ("dp", "sub"), "state", None), P("groups"))
    return jax.shard_map(shards, mesh=mesh, in_specs=in_specs, out_specs=out_specs, check_vma=False)
```

time: 685 us -> 533 us (0.78)
  waiting for transfers between devices: 351 us -> 32.9 us
  Pallas kernels: 0 us -> 117 us
  starting transfers between devices: 0.73 us -> 102 us
  matrix products: 70.2 us -> 0 us
  local copies, waits for them, and re-layouts: 77.5 us -> 23.8 us
  blocking collectives: 131 us -> 183 us
  other arithmetic: 38.9 us -> 66.9 us
  between operations: 14.2 us -> 5.33 us
    reduce_scatter x4 -> x0, waiting for transfers between devices: 291 us -> none  [shards(): lax.psum_scatter(mixed.reshape(seq_count, blocks, piece_len), 'state', sc...]
    all_gather x0 -> x8, blocking collectives: none -> 171 us  [shards(): lax.all_gather(own_sum[None], ('state', 'dp', 'sub'), axis=0, tiled=True)]
    psum x4 -> x0, blocking collectives: 131 us -> none  [shards(): lax.psum(jnp.sum(weighted, axis=(1, 2, 3)), ('state', 'dp', 'sub')) / H]
    pallas_call x0 -> x8, Pallas kernels: none -> 117 us  [product(): pl.pallas_call(functools.partial(product_kernel, len(xs), with_peak), gri...]
    ppermute x0 -> x72, starting transfers between devices: none -> 102 us  [the longest x24 69.8 us: line_sum(): lax.ppermute((to_r * scale).astype(jnp.float16), 'state', [(i, i + 1) for...]
    dot_general x4 -> x0, matrix products: 70.2 us -> none  [shards(): mixed = jnp.dot(left_side, weight_rows, preferred_element_type=jnp.float32)]
    all_gather x4 -> x0, waiting for transfers between devices: 59.4 us -> none  [shards(): shard_rows = lax.all_gather(lowered, ('dp', 'sub'), axis=1, tiled=True)]
    dot_general x1 -> x0, local copies, waits for them, and re-layouts: 41 us -> none  [shards(): mixed = jnp.dot(left_side, weight_rows, preferred_element_type=jnp.float32)]
  transfers between devices with their start and end apart: 8 -> 72, of which waited for: 7 -> 9; matrix products, arithmetic and copies ran while one was open for 9% -> 15% of each run, Pallas kernels for 0% -> 22%
where the time goes in v1:
time: 533 us; the launch traced here: 531 us
  blocking collectives  183 us (34%)
  Pallas kernels  117 us (22%)
  starting transfers between devices  102 us (19%)
  other arithmetic  66.9 us (13%)
  waiting for transfers between devices  32.9 us (6%)
  local copies, waits for them, and re-layouts  23.8 us (4%)
  between operations  5.33 us (1%)
    all_gather x8, blocking collectives, shards(): lax.all_gather(own_sum[None], ('state', 'dp', 'sub'), axis=0, tiled=True)  171 us
    pallas_call x8, Pallas kernels, product(): pl.pallas_call(functools.partial(product_kernel, len(xs), with_peak), gri...  117 us
    ppermute x24, starting transfers between devices, line_sum(): lax.ppermute((to_r * scale).astype(jnp.float16), 'state', [(i, i + 1) for...  69.8 us
    ppermute x24, waiting for transfers between devices, line_sum(): lax.ppermute((to_r * scale).astype(jnp.float16), 'state', [(i, i + 1) for...  25.5 us
    ppermute x24, starting transfers between devices, line_sum(): lax.ppermute((to_l * scale).astype(jnp.float16), 'state', [(i, i - 1) for...  24.2 us
    unnamed x44, local copies, waits for them, and re-layouts  23 us
    convert_element_type x24, other arithmetic, line_sum(): (to_r * scale).astype(jnp.float16)  21 us
    convert_element_type x6, other arithmetic, shards(): xs = gather_blocks(messages[h].astype(jnp.bfloat16))  12.1 us
  transfers between devices with their start and end apart: 72, of which 9 were waited for; matrix products, arithmetic and copies ran while one was open for 15% of the time, Pallas kernels for 22%

profile of v1, /device:TPU:0, one launch (start us, length us, event | category | flops | bytes accessed | tf_op | source)
XLA Modules:
  0.0 530.6 jit_solution(11727558156834948777)
XLA Ops:
  5.6 9.8 %copy.14 = bf16[4,256,1,4,1024]{4,1,3,0,2:T(8,128)(2,1)} copy(bf16[4,256,1,4,1024]{4,3,2,1,0:T(4,128)(2,1)} %param.4) | data formatting | bytes 16777216 | tf_op args[1]
  15.5 8.4 %fusion = bf16[4,4,256,1024]{3,2,1,0:T(8,128)(2,1)} fusion(s32[]{:T(128)S(6)} %select_n.12, bf16[4,4,256,1024]{3,2,1,0:T(8,128)(2,1)} %bitcast.354), kind=kLoop, calls=%fused_computation.2 | loop fusion | flops 4194304 | bytes 16777220 | tf_op jit(solution)/shard_map/concatenate | solution.py:117
  28.2 16.2 %product_peak.1 = (f32[4,128,1024]{2,1,0:T(8,128)S(1)}, f32[8,512]{1,0:T(8,128)S(1)}) custom-call(s32[5]{0:T(128)S(1)} %stack.38.idx_ref, bf16[128,1024]{1,0:T(8,128)(2,1)S(1)} %get-tuple-element.83.refs_0_, bf16[128,1024]{1,0:T(8,128)(2,1)S(1)} %collective-permute-done.refs_1_, bf16[128,1024]{1,0:T(8,128)(2,1)S(1)} %copy-done.8, ...), custom_call_target="tpu_custom_call" | custom-call | flops 4294967296 | bytes 33554432 | tf_op jit(solution)/shard_map/product_peak/pallas_call | solution.py:54
  50.9 12.1 %all-reduce = f32[4]{0:T(128)S(1)} all-reduce(f32[4]{0:T(128)S(1)} %dynamic-update-slice), channel_id=2, replica_groups=mesh['groups'=2,'state'=4,'dp'=2,'sub'=2] {'state'}, use_global_device_ids=true, to_apply=%add | all-reduce | flops 4 | bytes 32
  64.2 14.4 %product.7 = f32[4,128,1024]{2,1,0:T(8,128)S(1)} custom-call(s32[5]{0:T(128)S(1)} %stack.38.idx_ref, bf16[128,1024]{1,0:T(8,128)(2,1)S(1)} %get-tuple-element.82.refs_0_, bf16[128,1024]{1,0:T(8,128)(2,1)S(1)} %collective-permute-done.9.refs_1_, bf16[128,1024]{1,0:T(8,128)(2,1)S(1)} %collective-permute-done.10.refs_2_, ...), custom_call_target="tpu_custom_call" | custom-call | flops 4294967296 | bytes 33554432 | tf_op jit(solution)/shard_map/product/pallas_call | solution.py:54
  82.1 9.5 %slice_convert_fusion.1 = (f32[1,4,128,1024]{3,2,1,0:T(8,128)}, f32[1,4,128,1024]{3,2,1,0:T(8,128)}, f32[1,4,128,1024]{3,2,1,0:T(8,128)}, f32[1,4,128,1024]{3,2,...) fusion(bf16[4,4,256,1024]{3,2,1,0:T(8,128)(2,1)} %fusion), kind=kLoop, calls=%fused_computation.22 | loop fusion | flops 4194304 | bytes 25165824 | tf_op jit(solution)/shard_map/convert_element_type | solution.py:147
  103.3 18.8 %all-gather.9 = f32[16,1,128]{2,1,0:T(1,128)S(1)} all-gather(f32[1,1,128]{2,1,0:T(1,128)S(1)} %bitcast.362), channel_id=4, replica_groups=mesh['groups'=2,'state'=4,'dp'=2,'sub'=2] {'state','dp','sub'}, dimensions={0}, use_global_device_ids=true | all-gather | bytes 8704 | tf_op jit(solution)/shard_map/all_gather | solution.py:149
  141.4 24.8 %all-gather.8 = f32[16,1,128]{2,1,0:T(1,128)S(1)} all-gather(f32[1,1,128]{2,1,0:T(1,128)S(1)} %bitcast.356), channel_id=3, replica_groups=mesh['groups'=2,'state'=4,'dp'=2,'sub'=2] {'state','dp','sub'}, dimensions={0}, use_global_device_ids=true | all-gather | bytes 8704 | tf_op jit(solution)/shard_map/all_gather | solution.py:149
  169.0 14.3 %product.9 = f32[4,128,1024]{2,1,0:T(8,128)S(1)} custom-call(s32[5]{0:T(128)S(1)} %stack.38.idx_ref, bf16[128,1024]{1,0:T(8,128)(2,1)S(1)} %get-tuple-element.28.refs_0_, bf16[128,1024]{1,0:T(8,128)(2,1)S(1)} %collective-permute-done.27.refs_1_, bf16[128,1024]{1,0:T(8,128)(2,1)S(1)} %collective-permute-done.28.refs_2_, ...), custom_call_target="tpu_custom_call" | custom-call | flops 4294967296 | bytes 33554432 | tf_op jit(solution)/shard_map/product/pallas_call | solution.py:54
  198.2 14.3 %product.8 = f32[4,128,1024]{2,1,0:T(8,128)S(1)} custom-call(s32[5]{0:T(128)S(1)} %stack.38.idx_ref, bf16[128,1024]{1,0:T(8,128)(2,1)S(1)} %get-tuple-element.26.refs_0_, bf16[128,1024]{1,0:T(8,128)(2,1)S(1)} %collective-permute-done.18.refs_1_, bf16[128,1024]{1,0:T(8,128)(2,1)S(1)} %collective-permute-done.19.refs_2_, ...), custom_call_target="tpu_custom_call" | custom-call | flops 4294967296 | bytes 33554432 | tf_op jit(solution)/shard_map/product/pallas_call | solution.py:54
  222.4 25.0 %all-gather.11 = f32[16,1,128]{2,1,0:T(1,128)S(1)} all-gather(f32[1,1,128]{2,1,0:T(1,128)S(1)} %bitcast.358), channel_id=6, replica_groups=mesh['groups'=2,'state'=4,'dp'=2,'sub'=2] {'state','dp','sub'}, dimensions={0}, use_global_device_ids=true | all-gather | bytes 8704 | tf_op jit(solution)/shard_map/all_gather | solution.py:149
  256.6 5.4 %collective-permute-start.23 = (f16[128,1024]{1,0:T(8,128)(2,1)S(1)}, f16[128,1024]{1,0:T(8,128)(2,1)S(1)}, u32[]{:S(2)}, u32[]{:S(2)}) collective-permute-start(f16[128,1024]{1,0:T(8,128)(2,1)S(1)} %get-tuple-element.68), channel_id=1, source_target_pairs={{0,4},{4,8},{8,12},{1,5},{5,9},{9,13},{2,6},{6,10},{10,14},{3,7},{... | collective-permute-start | bytes 786440 | tf_op jit(solution)/shard_map/ppermute | solution.py:101
  263.3 19.6 %all-gather.10 = f32[16,1,128]{2,1,0:T(1,128)S(1)} all-gather(f32[1,1,128]{2,1,0:T(1,128)S(1)} %bitcast.357), channel_id=5, replica_groups=mesh['groups'=2,'state'=4,'dp'=2,'sub'=2] {'state','dp','sub'}, dimensions={0}, use_global_device_ids=true | all-gather | bytes 8704 | tf_op jit(solution)/shard_map/all_gather | solution.py:149
  285.8 14.3 %product.11 = f32[4,128,1024]{2,1,0:T(8,128)S(1)} custom-call(s32[5]{0:T(128)S(1)} %stack.38.idx_ref, bf16[128,1024]{1,0:T(8,128)(2,1)S(1)} %get-tuple-element.24.refs_0_, bf16[128,1024]{1,0:T(8,128)(2,1)S(1)} %collective-permute-done.45.refs_1_, bf16[128,1024]{1,0:T(8,128)(2,1)S(1)} %collective-permute-done.46.refs_2_, ...), custom_call_target="tpu_custom_call" | custom-call | flops 4294967296 | bytes 33554432 | tf_op jit(solution)/shard_map/product/pallas_call | solution.py:54
  313.1 14.4 %product.10 = f32[4,128,1024]{2,1,0:T(8,128)S(1)} custom-call(s32[5]{0:T(128)S(1)} %stack.38.idx_ref, bf16[128,1024]{1,0:T(8,128)(2,1)S(1)} %get-tuple-element.22.refs_0_, bf16[128,1024]{1,0:T(8,128)(2,1)S(1)} %collective-permute-done.36.refs_1_, bf16[128,1024]{1,0:T(8,128)(2,1)S(1)} %collective-permute-done.37.refs_2_, ...), custom_call_target="tpu_custom_call" | custom-call | flops 4294967296 | bytes 33554432 | tf_op jit(solution)/shard_map/product/pallas_call | solution.py:54
  338.5 25.0 %all-gather.13 = f32[16,1,128]{2,1,0:T(1,128)S(1)} all-gather(f32[1,1,128]{2,1,0:T(1,128)S(1)} %bitcast.359), channel_id=8, replica_groups=mesh['groups'=2,'state'=4,'dp'=2,'sub'=2] {'state','dp','sub'}, dimensions={0}, use_global_device_ids=true | all-gather | bytes 8704 | tf_op jit(solution)/shard_map/all_gather | solution.py:149
  372.3 5.4 %collective-permute-start.41 = (f16[128,1024]{1,0:T(8,128)(2,1)}, f16[128,1024]{1,0:T(8,128)(2,1)S(1)}, u32[]{:S(2)}, u32[]{:S(2)}) collective-permute-start(f16[128,1024]{1,0:T(8,128)(2,1)} %get-tuple-element.44), channel_id=1, source_target_pairs={{0,4},{4,8},{8,12},{1,5},{5,9},{9,13},{2,6},{6,10},{10,14},{3,7},{... | collective-permute-start | bytes 786440 | tf_op jit(solution)/shard_map/ppermute | solution.py:101
  380.1 18.7 %all-gather.12 = f32[16,1,128]{2,1,0:T(1,128)S(1)} all-gather(f32[1,1,128]{2,1,0:T(1,128)S(1)} %bitcast.355), channel_id=7, replica_groups=mesh['groups'=2,'state'=4,'dp'=2,'sub'=2] {'state','dp','sub'}, dimensions={0}, use_global_device_ids=true | all-gather | bytes 8704 | tf_op jit(solution)/shard_map/all_gather | solution.py:149
  401.1 14.3 %product.13 = f32[4,128,1024]{2,1,0:T(8,128)S(1)} custom-call(s32[5]{0:T(128)S(1)} %stack.38.idx_ref, bf16[128,1024]{1,0:T(8,128)(2,1)S(1)} %get-tuple-element.20.refs_0_, bf16[128,1024]{1,0:T(8,128)(2,1)S(1)} %collective-permute-done.63.refs_1_, bf16[128,1024]{1,0:T(8,128)(2,1)S(1)} %collective-permute-done.64.refs_2_, ...), custom_call_target="tpu_custom_call" | custom-call | flops 4294967296 | bytes 33554432 | tf_op jit(solution)/shard_map/product/pallas_call | solution.py:54
  428.4 14.4 %product.12 = f32[4,128,1024]{2,1,0:T(8,128)S(1)} custom-call(s32[5]{0:T(128)S(1)} %stack.38.idx_ref, bf16[128,1024]{1,0:T(8,128)(2,1)S(1)} %get-tuple-element.18.refs_0_, bf16[128,1024]{1,0:T(8,128)(2,1)S(1)} %collective-permute-done.54.refs_1_, bf16[128,1024]{1,0:T(8,128)(2,1)S(1)} %collective-permute-done.55.refs_2_, ...), custom_call_target="tpu_custom_call" | custom-call | flops 4294967296 | bytes 33554432 | tf_op jit(solution)/shard_map/product/pallas_call | solution.py:54
  452.0 21.7 %all-gather.15 = f32[16,1,128]{2,1,0:T(1,128)S(1)} all-gather(f32[1,1,128]{2,1,0:T(1,128)S(1)} %bitcast.361), channel_id=10, replica_groups=mesh['groups'=2,'state'=4,'dp'=2,'sub'=2] {'state','dp','sub'}, dimensions={0}, use_global_device_ids=true | all-gather | bytes 8704 | tf_op jit(solution)/shard_map/all_gather | solution.py:149
  473.7 17.3 %all-gather.14 = f32[16,1,128]{2,1,0:T(1,128)S(1)} all-gather(f32[1,1,128]{2,1,0:T(1,128)S(1)} %bitcast.360), channel_id=9, replica_groups=mesh['groups'=2,'state'=4,'dp'=2,'sub'=2] {'state','dp','sub'}, dimensions={0}, use_global_device_ids=true | all-gather | bytes 8704 | tf_op jit(solution)/shard_map/all_gather | solution.py:149
  506.7 6.3 %collective-permute-start.59 = (f16[128,1024]{1,0:T(8,128)(2,1)S(1)}, f16[128,1024]{1,0:T(8,128)(2,1)S(1)}, u32[]{:S(2)}, u32[]{:S(2)}) collective-permute-start(f16[128,1024]{1,0:T(8,128)(2,1)S(1)} %get-tuple-element.38), channel_id=1, source_target_pairs={{0,4},{4,8},{8,12},{1,5},{5,9},{9,13},{2,6},{6,10},{10,14},{3,7},{... | collective-permute-start | bytes 786440 | tf_op jit(solution)/shard_map/ppermute | solution.py:101
  524.2 6.3 %copy.10 = f32[4,256,1,1,1024]{4,3,2,1,0:T(1,128)} copy(f32[4,256,1,1,1024]{4,1,0,3,2:T(8,128)S(1)} %maximum_bitcast_fusion) | data formatting | bytes 8388608
  (248 shorter events, 174.5 us)
Async XLA Ops:
  5.2 59.0 %collective-permute-start.10 = (bf16[128,1024]{1,0:T(8,128)(2,1)S(1)}, bf16[128,1024]{1,0:T(8,128)(2,1)S(1)}, u32[]{:S(2)}, u32[]{:S(2)}) collective-permute-start(bf16[128,1024]{1,0:T(8,128)(2,1)S(1)} %get-tuple-element.82.refs_0_), channel_id=1, source_target_pairs={{0,1},{1,0},{2,3},{3,2},{4,5},{5,4},{6,7},{7,6},{8,9},{9,8},{10,11... | collective-permute-start | bytes 786440 | tf_op jit(solution)/shard_map/ppermute | solution.py:80
  24.6 39.6 %collective-permute-start.11 = (bf16[128,1024]{1,0:T(8,128)(2,1)S(1)}, bf16[128,1024]{1,0:T(8,128)(2,1)}, u32[]{:S(2)}, u32[]{:S(2)}) collective-permute-start(bf16[128,1024]{1,0:T(8,128)(2,1)S(1)} %collective-permute-done.9.refs_1_), channel_id=1, source_target_pairs={{0,1},{1,0},{2,3},{3,2},{4,5},{5,4},{6,7},{7,6},{8,9},{9,8},{10,11... | collective-permute-start | bytes 786440 | tf_op jit(solution)/shard_map/ppermute | solution.py:80
  47.3 46.1 %collective-permute-start.3 = (f16[128,1024]{1,0:T(8,128)(2,1)S(1)}, f16[128,1024]{1,0:T(8,128)(2,1)S(1)}, u32[]{:S(2)}, u32[]{:S(2)}) collective-permute-start(f16[128,1024]{1,0:T(8,128)(2,1)S(1)} %fusion.39), channel_id=1, source_target_pairs={{0,4},{1,5},{2,6},{3,7},{16,20},{17,21},{18,22},{19,23}} | collective-permute-start | bytes 786440 | tf_op jit(solution)/shard_map/ppermute | solution.py:101
  94.6 27.5 %collective-permute-start.4 = (f16[128,1024]{1,0:T(8,128)(2,1)S(1)}, f16[128,1024]{1,0:T(8,128)(2,1)S(1)}, u32[]{:S(2)}, u32[]{:S(2)}) collective-permute-start(f16[128,1024]{1,0:T(8,128)(2,1)S(1)} %fusion.43), channel_id=1, source_target_pairs={{0,4},{4,8},{1,5},{5,9},{2,6},{6,10},{3,7},{7,11},{16,20},{20,24},... | collective-permute-start | bytes 786440 | tf_op jit(solution)/shard_map/ppermute | solution.py:101
  97.8 27.1 %collective-permute-start.13 = (f16[128,1024]{1,0:T(8,128)(2,1)}, f16[128,1024]{1,0:T(8,128)(2,1)S(1)}, u32[]{:S(2)}, u32[]{:S(2)}) collective-permute-start(f16[128,1024]{1,0:T(8,128)(2,1)} %get-tuple-element.76), channel_id=1, source_target_pairs={{0,4},{4,8},{1,5},{5,9},{2,6},{6,10},{3,7},{7,11},{16,20},{20,24},... | collective-permute-start | bytes 786440 | tf_op jit(solution)/shard_map/ppermute | solution.py:101
  129.2 37.5 %collective-permute-start.5 = (f16[128,1024]{1,0:T(8,128)(2,1)}, f16[128,1024]{1,0:T(8,128)(2,1)S(1)}, u32[]{:S(2)}, u32[]{:S(2)}) collective-permute-start(f16[128,1024]{1,0:T(8,128)(2,1)} %get-tuple-element.80), channel_id=1, source_target_pairs={{0,4},{4,8},{8,12},{1,5},{5,9},{9,13},{2,6},{6,10},{10,14},{3,7},{... | collective-permute-start | bytes 786440 | tf_op jit(solution)/shard_map/ppermute | solution.py:101
  139.8 26.8 %collective-permute-start.27 = (bf16[128,1024]{1,0:T(8,128)(2,1)S(1)}, bf16[128,1024]{1,0:T(8,128)(2,1)S(1)}, u32[]{:S(2)}, u32[]{:S(2)}) collective-permute-start(bf16[128,1024]{1,0:T(8,128)(2,1)S(1)} %get-tuple-element.28.refs_0_), channel_id=1, source_target_pairs={{0,2},{2,0},{1,3},{3,1},{4,6},{6,4},{5,7},{7,5},{8,10},{10,8},{9,1... | collective-permute-start | bytes 786440 | tf_op jit(solution)/shard_map/ppermute | solution.py:76
  140.1 26.7 %collective-permute-start.8 = (f16[128,1024]{1,0:T(8,128)(2,1)S(1)}, f16[128,1024]{1,0:T(8,128)(2,1)S(1)}, u32[]{:S(2)}, u32[]{:S(2)}) collective-permute-start(f16[128,1024]{1,0:T(8,128)(2,1)S(1)} %fusion.41), channel_id=1, source_target_pairs={{4,0},{8,4},{12,8},{5,1},{9,5},{13,9},{6,2},{10,6},{14,10},{7,3},{... | collective-permute-start | bytes 786440 | tf_op jit(solution)/shard_map/ppermute | solution.py:102
  213.4 33.9 %collective-permute-start.21 = (f16[128,1024]{1,0:T(8,128)(2,1)}, f16[128,1024]{1,0:T(8,128)(2,1)S(1)}, u32[]{:S(2)}, u32[]{:S(2)}) collective-permute-start(f16[128,1024]{1,0:T(8,128)(2,1)} %get-tuple-element.72), channel_id=1, source_target_pairs={{0,4},{1,5},{2,6},{3,7},{16,20},{17,21},{18,22},{19,23}} | collective-permute-start | bytes 786440 | tf_op jit(solution)/shard_map/ppermute | solution.py:101
  216.0 31.4 %collective-permute-start.24 = (f16[128,1024]{1,0:T(8,128)(2,1)S(1)}, f16[128,1024]{1,0:T(8,128)(2,1)S(1)}, u32[]{:S(2)}, u32[]{:S(2)}) collective-permute-start(f16[128,1024]{1,0:T(8,128)(2,1)S(1)} %get-tuple-element.73), channel_id=1, source_target_pairs={{12,8},{13,9},{14,10},{15,11},{28,24},{29,25},{30,26},{31,27}} | collective-permute-start | bytes 786440 | tf_op jit(solution)/shard_map/ppermute | solution.py:102
  219.8 31.0 %collective-permute-start.32 = (f16[128,1024]{1,0:T(8,128)(2,1)}, f16[128,1024]{1,0:T(8,128)(2,1)S(1)}, u32[]{:S(2)}, u32[]{:S(2)}) collective-permute-start(f16[128,1024]{1,0:T(8,128)(2,1)} %get-tuple-element.62), channel_id=1, source_target_pairs={{0,4},{4,8},{8,12},{1,5},{5,9},{9,13},{2,6},{6,10},{10,14},{3,7},{... | collective-permute-start | bytes 786440 | tf_op jit(solution)/shard_map/ppermute | solution.py:101
  221.1 29.7 %collective-permute-start.35 = (f16[128,1024]{1,0:T(8,128)(2,1)}, f16[128,1024]{1,0:T(8,128)(2,1)S(1)}, u32[]{:S(2)}, u32[]{:S(2)}) collective-permute-start(f16[128,1024]{1,0:T(8,128)(2,1)} %get-tuple-element.63), channel_id=1, source_target_pairs={{4,0},{8,4},{12,8},{5,1},{9,5},{13,9},{6,2},{10,6},{14,10},{7,3},{... | collective-permute-start | bytes 786440 | tf_op jit(solution)/shard_map/ppermute | solution.py:102
  252.9 30.4 %collective-permute-start.45 = (bf16[128,1024]{1,0:T(8,128)(2,1)S(1)}, bf16[128,1024]{1,0:T(8,128)(2,1)S(1)}, u32[]{:S(2)}, u32[]{:S(2)}) collective-permute-start(bf16[128,1024]{1,0:T(8,128)(2,1)S(1)} %get-tuple-element.24.refs_0_), channel_id=1, source_target_pairs={{0,2},{2,0},{1,3},{3,1},{4,6},{6,4},{5,7},{7,5},{8,10},{10,8},{9,1... | collective-permute-start | bytes 786440 | tf_op jit(solution)/shard_map/ppermute | solution.py:76
  256.6 26.9 %collective-permute-start.23 = (f16[128,1024]{1,0:T(8,128)(2,1)S(1)}, f16[128,1024]{1,0:T(8,128)(2,1)S(1)}, u32[]{:S(2)}, u32[]{:S(2)}) collective-permute-start(f16[128,1024]{1,0:T(8,128)(2,1)S(1)} %get-tuple-element.68), channel_id=1, source_target_pairs={{0,4},{4,8},{8,12},{1,5},{5,9},{9,13},{2,6},{6,10},{10,14},{3,7},{... | collective-permute-start | bytes 786440 | tf_op jit(solution)/shard_map/ppermute | solution.py:101
  308.0 26.8 %collective-permute-start.49 = (f16[128,1024]{1,0:T(8,128)(2,1)S(1)}, f16[128,1024]{1,0:T(8,128)(2,1)S(1)}, u32[]{:S(2)}, u32[]{:S(2)}) collective-permute-start(f16[128,1024]{1,0:T(8,128)(2,1)S(1)} %get-tuple-element.58), channel_id=1, source_target_pairs={{0,4},{4,8},{1,5},{5,9},{2,6},{6,10},{3,7},{7,11},{16,20},{20,24},... | collective-permute-start | bytes 786440 | tf_op jit(solution)/shard_map/ppermute | solution.py:101
  328.3 35.2 %collective-permute-start.39 = (f16[128,1024]{1,0:T(8,128)(2,1)}, f16[128,1024]{1,0:T(8,128)(2,1)S(1)}, u32[]{:S(2)}, u32[]{:S(2)}) collective-permute-start(f16[128,1024]{1,0:T(8,128)(2,1)} %get-tuple-element.48), channel_id=1, source_target_pairs={{0,4},{1,5},{2,6},{3,7},{16,20},{17,21},{18,22},{19,23}} | collective-permute-start | bytes 786440 | tf_op jit(solution)/shard_map/ppermute | solution.py:101
  332.1 31.4 %collective-permute-start.42 = (f16[128,1024]{1,0:T(8,128)(2,1)S(1)}, f16[128,1024]{1,0:T(8,128)(2,1)S(1)}, u32[]{:S(2)}, u32[]{:S(2)}) collective-permute-start(f16[128,1024]{1,0:T(8,128)(2,1)S(1)} %get-tuple-element.49), channel_id=1, source_target_pairs={{12,8},{13,9},{14,10},{15,11},{28,24},{29,25},{30,26},{31,27}} | collective-permute-start | bytes 786440 | tf_op jit(solution)/shard_map/ppermute | solution.py:102
  335.9 29.8 %collective-permute-start.50 = (f16[128,1024]{1,0:T(8,128)(2,1)}, f16[128,1024]{1,0:T(8,128)(2,1)S(1)}, u32[]{:S(2)}, u32[]{:S(2)}) collective-permute-start(f16[128,1024]{1,0:T(8,128)(2,1)} %get-tuple-element.56), channel_id=1, source_target_pairs={{0,4},{4,8},{8,12},{1,5},{5,9},{9,13},{2,6},{6,10},{10,14},{3,7},{... | collective-permute-start | bytes 786440 | tf_op jit(solution)/shard_map/ppermute | solution.py:101
  337.2 28.5 %collective-permute-start.53 = (f16[128,1024]{1,0:T(8,128)(2,1)}, f16[128,1024]{1,0:T(8,128)(2,1)S(1)}, u32[]{:S(2)}, u32[]{:S(2)}) collective-permute-start(f16[128,1024]{1,0:T(8,128)(2,1)} %get-tuple-element.57), channel_id=1, source_target_pairs={{4,0},{8,4},{12,8},{5,1},{9,5},{13,9},{6,2},{10,6},{14,10},{7,3},{... | collective-permute-start | bytes 786440 | tf_op jit(solution)/shard_map/ppermute | solution.py:102
  368.1 31.2 %collective-permute-start.63 = (bf16[128,1024]{1,0:T(8,128)(2,1)S(1)}, bf16[128,1024]{1,0:T(8,128)(2,1)S(1)}, u32[]{:S(2)}, u32[]{:S(2)}) collective-permute-start(bf16[128,1024]{1,0:T(8,128)(2,1)S(1)} %get-tuple-element.20.refs_0_), channel_id=1, source_target_pairs={{0,2},{2,0},{1,3},{3,1},{4,6},{6,4},{5,7},{7,5},{8,10},{10,8},{9,1... | collective-permute-start | bytes 786440 | tf_op jit(solution)/shard_map/ppermute | solution.py:76
  372.3 27.1 %collective-permute-start.41 = (f16[128,1024]{1,0:T(8,128)(2,1)}, f16[128,1024]{1,0:T(8,128)(2,1)S(1)}, u32[]{:S(2)}, u32[]{:S(2)}) collective-permute-start(f16[128,1024]{1,0:T(8,128)(2,1)} %get-tuple-element.44), channel_id=1, source_target_pairs={{0,4},{4,8},{8,12},{1,5},{5,9},{9,13},{2,6},{6,10},{10,14},{3,7},{... | collective-permute-start | bytes 786440 | tf_op jit(solution)/shard_map/ppermute | solution.py:101
  423.3 27.7 %collective-permute-start.67 = (f16[128,1024]{1,0:T(8,128)(2,1)S(1)}, f16[128,1024]{1,0:T(8,128)(2,1)S(1)}, u32[]{:S(2)}, u32[]{:S(2)}) collective-permute-start(f16[128,1024]{1,0:T(8,128)(2,1)S(1)} %get-tuple-element.52), channel_id=1, source_target_pairs={{0,4},{4,8},{1,5},{5,9},{2,6},{6,10},{3,7},{7,11},{16,20},{20,24},... | collective-permute-start | bytes 786440 | tf_op jit(solution)/shard_map/ppermute | solution.py:101
  443.8 49.9 %collective-permute-start.57 = (f16[128,1024]{1,0:T(8,128)(2,1)}, f16[128,1024]{1,0:T(8,128)(2,1)S(1)}, u32[]{:S(2)}, u32[]{:S(2)}) collective-permute-start(f16[128,1024]{1,0:T(8,128)(2,1)} %get-tuple-element.42), channel_id=1, source_target_pairs={{0,4},{1,5},{2,6},{3,7},{16,20},{17,21},{18,22},{19,23}} | collective-permute-start | bytes 786440 | tf_op jit(solution)/shard_map/ppermute | solution.py:101
  447.5 46.1 %collective-permute-start.60 = (f16[128,1024]{1,0:T(8,128)(2,1)}, f16[128,1024]{1,0:T(8,128)(2,1)}, u32[]{:S(2)}, u32[]{:S(2)}) collective-permute-start(f16[128,1024]{1,0:T(8,128)(2,1)} %get-tuple-element.43), channel_id=1, source_target_pairs={{12,8},{13,9},{14,10},{15,11},{28,24},{29,25},{30,26},{31,27}} | collective-permute-start | bytes 786440 | tf_op jit(solution)/shard_map/ppermute | solution.py:102
  (67 other events, 748.6 us)
